TPU v7x, 256 devices: a whole 4x4x8 slice. The times are simulated.
256 devices in a mesh: aux: 4 (over x), row: 16 (over z_hi, y), col: 4 (over z_lo, core).
Axes of the slice: x: 4, y: 4, z: 8 (z_hi: 4, z_lo: 2; z = z_hi * 2 + z_lo), core: 2. Of those that a mesh axis runs over, the one named last changes fastest.
Arguments:
- factors: bfloat16 [8, 4, 2560, 10240], P('aux', None, 'row', 'col'), may hold values from -0.078125 to 0.078125
- orbitals: bfloat16 [10240, 512], P('col'), may hold values from -0.25 to 0.25
- tile_mask: int32 [8, 80, 80], P('aux'), may hold values from 0 to 1, as said below
Outputs:
- exchange: float32 [10240, 10240], P(('aux', 'row'), 'col')
Inputs may be any that keep to these rules, and one draw needn't show every extreme that they name: `tile_mask`: 0 or 1; present tiles cluster around a centre tile drawn for each auxiliary function, and absent tiles occur everywhere.
All inputs are finite; a program needn't handle non-finite values.
Results may differ from a plain program's by a relative error of at most 0.02.
Values may be sent and summed in bfloat16 or wider, within the bound.
A program may use at most 64 MiB of HBM per device.

v0:
```python
import jax
import jax.numpy as jnp
from jax import lax
from jax.sharding import PartitionSpec as P

NB = 10240
TILE = 128


def on_device(factors, orbitals, tile_mask):
    local_count = factors.shape[0]
    aux_parts = factors.shape[1]
    row_len = factors.shape[2]
    col_len = factors.shape[3]
    occ_count = orbitals.shape[1]
    row_index = lax.axis_index("row")
    col_index = lax.axis_index("col")
    tile_cols = col_len // TILE
    basis_rows = (
        jnp.arange(aux_parts, dtype=jnp.int32)[:, None] * (NB // aux_parts)
        + row_index * row_len
        + jnp.arange(row_len, dtype=jnp.int32)[None, :]
    ) // TILE
    row_tiles = jnp.take(tile_mask, basis_rows, axis=1)
    local_tiles = lax.dynamic_slice_in_dim(row_tiles, col_index * tile_cols, tile_cols, axis=3)
    masked = (
        factors.reshape(local_count, aux_parts, row_len, tile_cols, TILE)
        * local_tiles.astype(jnp.bfloat16)[..., None]
    )
    masked = masked.reshape(factors.shape)
    partial_orb = jnp.einsum("qatn,nk->atqk", masked, orbitals, preferred_element_type=jnp.float32)
    own_panel = lax.psum_scatter(
        partial_orb.astype(jnp.bfloat16), "col", scatter_dimension=0, tiled=True
    )
    row_panel = lax.all_gather(own_panel, "col", axis=0, tiled=True)
    rows_three = row_panel.reshape(aux_parts * row_len, local_count, occ_count)
    cols_three = own_panel.reshape(row_len, local_count, occ_count)
    zeros_k = jnp.zeros((aux_parts * row_len, col_len), jnp.float32)

    def one_function(function_index, summed):
        left_rows = lax.dynamic_index_in_dim(rows_three, function_index, 1, keepdims=False)
        right_rows = lax.dynamic_index_in_dim(cols_three, function_index, 1, keepdims=False)
        return summed + lax.dot_general(
            left_rows,
            lax.all_gather(right_rows, "row", axis=0, tiled=True),
            (((1,), (1,)), ((), ())),
            preferred_element_type=jnp.float32,
        )

    partial_k = lax.fori_loop(0, local_count, one_function, zeros_k)
    return lax.psum_scatter(
        partial_k.astype(jnp.bfloat16), "aux", scatter_dimension=0, tiled=True
    ).astype(jnp.float32)


def solution(mesh):
    placed = (P("aux", None, "row", "col"), P("col", None), P("aux", None, None))
    return jax.shard_map(
        on_device, mesh=mesh, in_specs=placed, out_specs=P(("aux", "row"), "col"), check_vma=False
    )
```

profile of v0, /device:TPU:2, one launch (start us, length us, event | category | flops | bytes accessed | tf_op | source)
XLA Modules:
  0.0 318.5 jit_solution(14469421907034454084)
XLA Ops:
  6.5 0.0 copy-start
  6.5 0.0 all-reduce.3.cloned.1.call-start
  6.5 0.1 compare_select_fusion
  6.6 0.1 compare_and_fusion
  6.7 0.1 reshape.123
  6.8 3.4 %gather_fusion = s32[640,2,80]{2,0,1:T(8,128)S(1)} fusion(s32[2,80,80]{2,1,0:T(8,128)} %param.7, s32[1024]{0:T(1024)S(1)} %pad_clamp_fusion), kind=kCustom, calls=%fused_computation | custom fusion | bytes 821760 | tf_op jit(solution)/shard_map/jit(_take)/gather | solution.py:24
  10.2 0.3 fusion.18
  10.5 6.8 %mul.28 = bf16[2,4,160,20,128]{4,3,2,1,0:T(8,128)(2,1)} broadcast(bf16[2,4,160,20]{3,2,1,0:T(8,128)(2,1)S(1)} %fusion.18), dimensions={0,1,2,3} | broadcast | bytes 6604800 | tf_op jit(solution)/shard_map/mul | solution.py:27
  17.3 12.0 %mul.29 = bf16[2,4,160,2560]{3,2,1,0:T(8,128)(2,1)} reshape(bf16[2,4,160,20,128]{4,3,2,1,0:T(8,128)(2,1)} %mul.28) | data formatting | bytes 13107200 | tf_op jit(solution)/shard_map/mul | solution.py:27
  29.3 0.0 copy-done
  29.3 0.0 copy-start.1
  29.3 9.4 %fusion.12 = bf16[4,160,2,512]{3,1,0,2:T(8,128)(2,1)} fusion(bf16[2560,512]{1,0:T(8,128)(2,1)S(1)} %copy-done, bf16[2,4,160,2560]{3,2,1,0:T(8,128)(2,1)} %param.5, bf16[2,4,160,2560]{3,2,1,0:T(8,128)(2,1)} %mul.29), kind=kOutput, calls=%fused_computation.11 | convolution fusion | flops 3359375360 | bytes 17039360 | tf_op jit(solution)/shard_map/qatn,nk->atqk/dot_general | solution.py:31
  38.6 0.0 all-reduce.3.cloned.1.call-update
  38.7 0.0 all-gather.7.cloned.1.call-start
  38.7 0.0 copy-done.1
  38.7 0.6 dynamic-slice.1
  39.3 52.1 %all-reduce.3.cloned.1.call-done = bf16[4,160,2,512]{3,1,0,2:T(8,128)(2,1)} async-done(((bf16[4,160,2,512]{3,1,0,2:T(8,128)(2,1)}), bf16[4,160,2,512]{3,1,0,2:T(8,128)(2,1)}) %all-reduce.3.cloned.1.call-update) | async-done | bytes 1310736
  91.5 2.4 constant_dynamic-slice_fusion.1
  93.8 0.0 all-gather.7.cloned.1.call-update
  93.9 1.6 fusion.25
  95.5 24.1 %all-gather.7.cloned.1.call-done = bf16[4,160,2,512]{3,1,0,2:T(8,128)(2,1)} async-done(((bf16[1,160,2,512]{3,1,0,2:T(8,128)(2,1)}), bf16[4,160,2,512]{3,1,0,2:T(8,128)(2,1)}) %all-gather.7.cloned.1.call-update) | async-done | bytes 1310736 | tf_op jit(solution)/shard_map/all_gather | solution.py:35
  119.6 146.2 %while.14 = (s32[]{:T(128)}, f32[640,2560]{1,0:T(8,128)}, bf16[640,2,512]{2,0,1:T(8,128)(2,1)}, bf16[160,2,512]{2,0,1:T(8,128)(2,1)S(1)}, s32[]{:T(128)}, /*index=5*/s32[]{:T(128)}) while((s32[]{:T(128)}, f32[640,2560]{1,0:T(8,128)}, bf16[640,2,512]{2,0,1:T(8,128)(2,1)}, bf16[160,2,512]{2,0,1:T(8,128)(2,1)S(1)}, s32[]{:T(128)}, ...), condition=%wide.region_2.3_spmd.clone, body=%wide.region_1.2_spmd.clone.sunk | while | flops 1680998400 | bytes 25067656 | solution.py:50
  119.6 0.0 all-gather.9.cloned.1.call-start
  119.6 0.7 constant_dynamic-slice_fusion.3
  120.3 0.0 all-gather.9.cloned.1.call-update
  120.3 66.2 %all-gather.9.cloned.1.call-done = bf16[2560,1,512]{2,0,1:T(8,128)(2,1)} async-done(((bf16[160,1,512]{2,0,1:T(8,128)(2,1)}), bf16[2560,1,512]{2,0,1:T(8,128)(2,1)}) %all-gather.9.cloned.1.call-update) | async-done | bytes 2621456 | tf_op jit(solution)/shard_map/while/body/eval_jaxpr/all_gather | solution.py:45
  186.5 6.6 %select_add_fusion.2 = f32[640,2560]{1,0:T(8,128)} fusion(f32[640,2560]{1,0:T(8,128)} %get-tuple-element.144, pred[]{:T(512)S(6)} %compare.17, bf16[2560,1,512]{2,0,1:T(8,128)(2,1)} %all-gather.9.cloned.1.call-done, bf16[640,2,512]{2,0,1:T(8,128)(2,1)} %get-tuple-element.151, s32[]{:T(128)S(6)} %copy.12), kind=kOutput, calls=%fused_computation.1.clone.1 | convolution fusion | flops 1680998400 | bytes 16384005 | tf_op jit(solution)/shard_map/while/body/eval_jaxpr/dot_general | solution.py:43
  193.1 0.0 all-gather.9.cloned.1.call-start
  193.1 0.7 constant_dynamic-slice_fusion.3
  193.8 0.0 all-gather.9.cloned.1.call-update
  193.8 63.4 %all-gather.9.cloned.1.call-done = bf16[2560,1,512]{2,0,1:T(8,128)(2,1)} async-done(((bf16[160,1,512]{2,0,1:T(8,128)(2,1)}), bf16[2560,1,512]{2,0,1:T(8,128)(2,1)}) %all-gather.9.cloned.1.call-update) | async-done | bytes 2621456 | tf_op jit(solution)/shard_map/while/body/eval_jaxpr/all_gather | solution.py:45
  257.3 8.5 %select_add_fusion.2 = f32[640,2560]{1,0:T(8,128)} fusion(f32[640,2560]{1,0:T(8,128)} %get-tuple-element.144, pred[]{:T(512)S(6)} %compare.17, bf16[2560,1,512]{2,0,1:T(8,128)(2,1)} %all-gather.9.cloned.1.call-done, bf16[640,2,512]{2,0,1:T(8,128)(2,1)} %get-tuple-element.151, s32[]{:T(128)S(6)} %copy.12), kind=kOutput, calls=%fused_computation.1.clone.1 | convolution fusion | flops 1680998400 | bytes 16384005 | tf_op jit(solution)/shard_map/while/body/eval_jaxpr/dot_general | solution.py:43
  265.8 0.0 reduce-scatter.5.cloned.1.call-start
  265.8 5.0 %convert_element_type.18 = bf16[640,2560]{1,0:T(8,128)(2,1)} convert(f32[640,2560]{1,0:T(8,128)} %get-tuple-element.84) | non-fusion elementwise | flops 1638400 | bytes 9830400 | tf_op jit(solution)/shard_map/convert_element_type | solution.py:52
  270.7 0.0 reduce-scatter.5.cloned.1.call-update
  270.8 38.7 %reduce-scatter.5.cloned.1.call-done = bf16[160,2560]{1,0:T(8,128)(2,1)} async-done(((bf16[640,2560]{1,0:T(8,128)(2,1)}), bf16[160,2560]{1,0:T(8,128)(2,1)}) %reduce-scatter.5.cloned.1.call-update) | async-done | bytes 819216 | tf_op jit(solution)/shard_map/reduce_scatter | solution.py:51
  309.4 2.5 convert_element_type.19
  (3 shorter events, 0.0 us)
Async XLA Ops:
  6.5 22.7 %copy-start = (bf16[2560,512]{1,0:T(8,128)(2,1)S(1)}, bf16[2560,512]{1,0:T(8,128)(2,1)}, u32[]{:S(2)}) copy-start(bf16[2560,512]{1,0:T(8,128)(2,1)} %param.6) | copy-start | bytes 7864324
  6.5 84.9 %all-reduce.3.cloned.1.call-start = ((), (), s32[]{:S(2)}) async-start(), calls=%async_computation.3 | async-start | bytes 2621440
  29.3 9.4 %copy-start.1 = (u32[256]{0:T(256)S(1)}, u32[256]{0:T(256)}, u32[]{:S(2)}) copy-start(u32[256]{0:T(256)} %constant.82) | copy-start | bytes 3076
  38.7 80.9 %all-gather.7.cloned.1.call-start = ((), (), s32[]{:S(2)}) async-start(), calls=%async_computation.1 | async-start | bytes 1638400 | tf_op jit(solution)/shard_map/all_gather | solution.py:35
  119.6 66.9 %all-gather.9.cloned.1.call-start = ((), (), s32[]{:S(2)}) async-start(), calls=%async_computation.4 | async-start | bytes 2785280 | tf_op jit(solution)/shard_map/while/body/eval_jaxpr/all_gather | solution.py:45
  193.1 64.2 %all-gather.9.cloned.1.call-start = ((), (), s32[]{:S(2)}) async-start(), calls=%async_computation.4 | async-start | bytes 2785280 | tf_op jit(solution)/shard_map/while/body/eval_jaxpr/all_gather | solution.py:45
  265.8 43.7 %reduce-scatter.5.cloned.1.call-start = ((), (), s32[]{:S(2)}) async-start(), calls=%async_computation.2 | async-start | bytes 4096000 | tf_op jit(solution)/shard_map/reduce_scatter | solution.py:51
Sparse Core Ops, SparseCore 0:
  38.8 52.6 all-reduce.2
  94.0 25.5 all-gather.6
  122.8 63.6 all-gather.8
  196.0 61.1 all-gather.8
  270.9 38.5 reduce-scatter.4
where the time goes:
time: 321 us; the launch traced here: 318 us
  waiting for transfers between devices  245 us (76%)
  local copies, waits for them, and re-layouts  28.2 us (9%)
  matrix products  24.5 us (8%)
  between operations  13.2 us (4%)
  other arithmetic  7.97 us (2%)
    all_gather x2, waiting for transfers between devices, one_function(): lax.all_gather(right_rows, 'row', axis=0, tiled=True)  130 us
    unnamed x4, waiting for transfers between devices  52.2 us
    reduce_scatter x1, waiting for transfers between devices, on_device(): lax.psum_scatter(partial_k.astype(jnp.bfloat16), 'aux', scatter_dimension...  38.7 us
    all_gather x1, waiting for transfers between devices, on_device(): row_panel = lax.all_gather(own_panel, 'col', axis=0, tiled=True)  24.1 us
    mul x2, local copies, waits for them, and re-layouts, on_device(): factors.reshape(local_count, aux_parts, row_len, tile_cols, TILE)  18.7 us
    dot_general x2, matrix products, one_function(): lax.dot_general(left_rows, lax.all_gather(right_rows, 'row', axis=0, tile...  15.1 us
    dot_general x1, matrix products, on_device(): jnp.einsum('qatn,nk->atqk', masked, orbitals, preferred_element_type=jnp....  9.36 us
  transfers between devices with their start and end apart: 5, of which 5 were waited for; matrix products, arithmetic and copies ran while one was open for 1% of the time, Pallas kernels for 0%

commit v1 on v0

v1 whole, which is shorter than its diff:
```python
import jax
import jax.numpy as jnp
from jax import lax
from jax.experimental import pallas as pl
from jax.experimental.pallas import tpu as pltpu
from jax.sharding import PartitionSpec as P

NB = 10240
TILE = 128
MESH = pl.DeviceIdType.MESH
BF = jnp.bfloat16
F32 = jnp.float32
NT = (((1,), (1,)), ((), ()))
NX, NY, NZ = 4, 4, 4
ROWS, HALF, OCC = 160, 80, 512
WIDE = NY * ROWS
COLS = NB // 4
LAYERS = (0, 1, 3, 2)
N_SEMS = 80


def kernel(mask_ref, factors_ref, orbitals_ref, out_ref,
           fbuf, cbuf, mexp, masked, give, keep, got_a, put_b, got_b, panels, left, prod,
           far, near, got_far, got_near, held, in_sem, send_sem, recv_sem):
    x = lax.axis_index("aux")
    row = lax.axis_index("row")
    col = lax.axis_index("col")
    zh, y = lax.div(row, NY), lax.rem(row, NY)
    core_col = col + 1 - 2 * lax.rem(col, 2)
    pair_col = lax.rem(col + 2, 4)
    cross_col = 3 - col

    def at_x(d):
        return lax.rem(x + d + NX, NX)

    def at_y(d):
        return lax.rem(y + d + NY, NY)

    def at_z(d):
        return lax.rem(zh + d + NZ, NZ)

    core = {"col": core_col}
    pair = {"col": pair_col}
    y_dev = {d: {"row": zh * NY + at_y(d)} for d in (1, -1)}
    z_dev = {d: {"row": at_z(d) * NY + y} for d in (1, -1)}
    x_dev = {d: {"aux": at_x(d)} for d in (1, -1)}

    barrier = pltpu.get_barrier_semaphore()
    partners = [core, pair, y_dev[1], y_dev[-1], z_dev[1], z_dev[-1], x_dev[1], x_dev[-1]]
    for partner in partners:
        pl.semaphore_signal(barrier, inc=1, device_id=partner, device_id_type=MESH)

    order = (cross_col, pair_col, core_col, col)
    loads = {}
    load = pltpu.make_async_copy(orbitals_ref, cbuf, in_sem.at[8])
    load.start()
    for n, (q, s) in enumerate(((0, 0), (0, 1), (1, 0), (1, 1), (0, 2), (0, 3), (1, 2), (1, 3))):
        piece = pltpu.make_async_copy(factors_ref.at[q, order[s]], fbuf.at[q, order[s]], in_sem.at[n])
        piece.start()
        loads[q, s] = piece

    pick_row = lax.broadcasted_iota(jnp.int32, (64, 80), 0)
    pick_col = lax.broadcasted_iota(jnp.int32, (64, 80), 1)
    tile_row = (pick_row // 16) * (COLS // TILE) + (row * (ROWS // 32) + pick_row % 8) // (TILE // 32)
    spread_row = lax.broadcasted_iota(jnp.int32, (80, COLS), 0)
    spread_col = lax.broadcasted_iota(jnp.int32, (80, COLS), 1)
    spread = (spread_row == col * (COLS // TILE) + spread_col // TILE).astype(BF)
    flags = jnp.zeros((64, 80), F32)
    for q in range(2):
        pick = ((pick_col == tile_row) & ((pick_row % 16) // 8 == q)).astype(BF)
        flags = flags + jnp.dot(pick, mask_ref[q].astype(F32).astype(BF), preferred_element_type=F32)
    mexp[...] = jnp.dot(flags.astype(BF), spread, preferred_element_type=F32).reshape(4, 16, COLS)

    sends = []
    used = [0]

    def sem():
        used[0] += 1
        return used[0] - 1

    def send(src, dst, index, to):
        copy = pltpu.make_async_remote_copy(
            src_ref=src, dst_ref=dst, send_sem=send_sem.at[index], recv_sem=recv_sem.at[index],
            device_id=to, device_id_type=MESH)
        copy.start()
        sends.append(copy)

    def arrived(dst, index, to):
        pltpu.make_async_remote_copy(
            src_ref=dst, dst_ref=dst, send_sem=send_sem.at[index], recv_sem=recv_sem.at[index],
            device_id=to, device_id_type=MESH).wait_recv()

    s_a = {(q, s): sem() for q in range(2) for s in range(2)}
    s_b = {q: sem() for q in range(2)}
    s_pair = {q: sem() for q in range(2)}
    s_core = {q: sem() for q in range(2)}
    s_cross = {q: sem() for q in range(2)}
    s_z1 = {(q, d): sem() for q in range(2) for d in (1, -1)}
    s_z2 = {(q, d): sem() for q in range(2) for d in (1, -1)}
    s_y1 = {(n, q, d): sem() for n in range(NZ) for q in range(2) for d in (1, -1)}
    s_y2 = {(n, q, d): sem() for n in range(NZ) for q in range(2) for d in (1, -1)}
    s_far = {(i, d): sem() for i in range(NZ) for d in (1, -1)}
    s_near = {(i, d, h): sem() for i in range(NZ) for d in (1, -1) for h in range(2)}

    def partial_product(q, s):
        quarter = order[s]
        loads[q, s].wait()
        for g in range(ROWS // 32):
            flag_row = mexp[quarter, pl.ds(8 * q + g, 1), :].astype(BF)
            masked[pl.ds(32 * g, 32), :] = fbuf[q, quarter, pl.ds(32 * g, 32), :] * flag_row
        return jnp.dot(masked[...], cbuf[...], preferred_element_type=F32)

    def give_core(q, n):
        give[q, n] = partial_product(q, 2 * n).astype(BF)
        send(give.at[q, n], got_a.at[q, n], s_a[q, n], core)

    def give_pair(q):
        arrived(got_a.at[q, 0], s_a[q, 0], core)
        put_b[q] = (keep[q, 0] + got_a[q, 0].astype(F32)).astype(BF)
        send(put_b.at[q], got_b.at[q], s_b[q], pair)

    def finish_rows(q):
        arrived(got_a.at[q, 1], s_a[q, 1], core)
        arrived(got_b.at[q], s_b[q], pair)
        rows = (keep[q, 1] + got_a[q, 1].astype(F32) + got_b[q].astype(F32)).astype(BF)
        panels[zh, q, y] = rows
        left[q, col] = rows
        own = panels.at[zh, q, y]
        send(left.at[q, col], left.at[q, col], s_pair[q], pair)
        for d in (1, -1):
            send(own, own, s_y1[0, q, d], y_dev[d])
        for d in (1, -1):
            send(own, own, s_z1[q, d], z_dev[d])
        send(left.at[q, col], left.at[q, col], s_core[q], core)

    load.wait()
    give_value = partial_product(0, 0).astype(BF)
    give[0, 0] = give_value
    pl.semaphore_wait(barrier, len(partners))
    send(give.at[0, 0], got_a.at[0, 0], s_a[0, 0], core)
    keep[0, 0] = partial_product(0, 1)
    give_core(1, 0)
    give_pair(0)
    keep[1, 0] = partial_product(1, 1)
    give_core(0, 1)
    give_pair(1)
    keep[0, 1] = partial_product(0, 3)
    give_core(1, 1)
    keep[1, 1] = partial_product(1, 3)

    halves = {1: pl.ds(0, HALF), -1: pl.ds(HALF, HALF)}

    def along_y1(n, q):
        own = panels.at[at_z(LAYERS[n]), q, y]
        for d in (1, -1):
            send(own, own, s_y1[n, q, d], y_dev[d])

    def along_y2(n, q):
        for d in (1, -1):
            block = panels.at[at_z(LAYERS[n]), q, at_y(-d)]
            arrived(block, s_y1[n, q, d], y_dev[-d])
            part = panels.at[at_z(LAYERS[n]), q, at_y(-d), halves[d]]
            send(part, part, s_y2[n, q, d], y_dev[d])

    def along_z2(q):
        for d in (1, -1):
            block = panels.at[at_z(-d), q, y]
            arrived(block, s_z1[q, d], z_dev[-d])
            part = panels.at[at_z(-d), q, y, halves[d]]
            send(part, part, s_z2[q, d], z_dev[d])

    def end_z(q):
        for d in (1, -1):
            arrived(panels.at[at_z(2), q, y, halves[d]], s_z2[q, d], z_dev[-d])

    def pass_cross(q):
        arrived(left.at[q, pair_col], s_pair[q], pair)
        send(left.at[q, pair_col], left.at[q, pair_col], s_cross[q], core)

    def end_y(n):
        for q in range(2):
            for d in (1, -1):
                arrived(panels.at[at_z(LAYERS[n]), q, at_y(2), halves[d]], s_y2[n, q, d], y_dev[-d])

    def end_left():
        for q in range(2):
            arrived(left.at[q, core_col], s_core[q], core)
            arrived(left.at[q, cross_col], s_cross[q], core)

    def product(n):
        layer = at_z(LAYERS[n])
        value = jnp.zeros((4 * ROWS, WIDE), F32)
        for q in range(2):
            value = value + lax.dot_general(
                left[q].reshape(4 * ROWS, OCC), panels[layer, q].reshape(WIDE, OCC), NT,
                preferred_element_type=F32)
        prod[...] = value.reshape(4, ROWS, WIDE)
        far[n] = prod[at_x(2)].astype(BF)
        for d in (1, -1):
            send(far.at[n, halves[d]], got_far.at[n, 0 if d == 1 else 1], s_far[n, d], x_dev[d])
        for d in (1, -1):
            slot = 0 if d == 1 else 1
            mine, other = halves[d], halves[-d]
            near[n, slot, other] = prod[at_x(d), other].astype(BF)
            held[n, slot] = prod[at_x(d), mine]
            send(near.at[n, slot, other], got_near.at[n, slot, other], s_near[n, d, 1], x_dev[d])
        out_ref[layer] = prod[x]

    def pass_on(n):
        for d in (1, -1):
            slot = 0 if d == 1 else 1
            mine = halves[d]
            arrived(got_far.at[n, slot], s_far[n, d], x_dev[-d])
            near[n, slot, mine] = (held[n, slot] + got_far[n, slot].astype(F32)).astype(BF)
            send(near.at[n, slot, mine], got_near.at[n, slot, mine], s_near[n, d, 0], x_dev[d])

    def finish(n):
        layer = at_z(LAYERS[n])
        for d in (1, -1):
            slot = 0 if d == 1 else 1
            arrived(got_near.at[n, slot, halves[d]], s_near[n, d, 0], x_dev[-d])
            arrived(got_near.at[n, slot, halves[-d]], s_near[n, d, 1], x_dev[-d])
        out_ref[layer] += got_near[n, 0].astype(F32) + got_near[n, 1].astype(F32)

    finish_rows(0)
    finish_rows(1)
    along_y2(0, 0)
    along_y2(0, 1)
    pass_cross(0)
    along_z2(0)
    along_y1(1, 0)
    along_y1(2, 0)
    pass_cross(1)
    end_left()
    end_y(0)
    product(0)
    along_z2(1)
    along_y1(1, 1)
    along_y1(2, 1)
    pass_on(0)
    along_y2(1, 0)
    along_y2(2, 0)
    end_z(0)
    along_y1(3, 0)
    along_y2(1, 1)
    along_y2(2, 1)
    end_z(1)
    along_y1(3, 1)
    finish(0)
    end_y(1)
    product(1)
    end_y(2)
    product(2)
    along_y2(3, 0)
    pass_on(1)
    pass_on(2)
    along_y2(3, 1)
    finish(1)
    finish(2)
    end_y(3)
    product(3)
    pass_on(3)
    finish(3)
    for copy in sends:
        copy.wait_send()


def on_device(factors, orbitals, tile_mask):
    vmem = pl.BlockSpec(memory_space=pltpu.VMEM)
    hbm = pl.BlockSpec(memory_space=pl.ANY)
    out = pl.pallas_call(
        kernel,
        out_shape=jax.ShapeDtypeStruct((NZ, ROWS, WIDE), F32),
        in_specs=[vmem, hbm, hbm],
        out_specs=vmem,
        scratch_shapes=[
            pltpu.VMEM((2, 4, ROWS, COLS), BF),
            pltpu.VMEM((COLS, OCC), BF),
            pltpu.VMEM((4, 16, COLS), F32),
            pltpu.VMEM((ROWS, COLS), BF),
            pltpu.VMEM((2, 2, ROWS, OCC), BF),
            pltpu.VMEM((2, 2, ROWS, OCC), F32),
            pltpu.VMEM((2, 2, ROWS, OCC), BF),
            pltpu.VMEM((2, ROWS, OCC), BF),
            pltpu.VMEM((2, ROWS, OCC), BF),
            pltpu.VMEM((NZ, 2, NY, ROWS, OCC), BF),
            pltpu.VMEM((2, 4, ROWS, OCC), BF),
            pltpu.VMEM((4, ROWS, WIDE), F32),
            pltpu.VMEM((NZ, ROWS, WIDE), BF),
            pltpu.VMEM((NZ, 2, ROWS, WIDE), BF),
            pltpu.VMEM((NZ, 2, HALF, WIDE), BF),
            pltpu.VMEM((NZ, 2, ROWS, WIDE), BF),
            pltpu.VMEM((NZ, 2, HALF, WIDE), F32),
            pltpu.SemaphoreType.DMA((9,)),
            pltpu.SemaphoreType.DMA((N_SEMS,)),
            pltpu.SemaphoreType.DMA((N_SEMS,)),
        ],
        compiler_params=pltpu.CompilerParams(
            collective_id=0, has_side_effects=True, vmem_limit_bytes=56 * 2**20),
        cost_estimate=pl.CostEstimate(flops=7 * 10**9, bytes_accessed=12 * 10**6, transcendentals=0),
        name="exchange",
    )(tile_mask, factors, orbitals)
    return out.transpose(1, 0, 2).reshape(ROWS, NZ * WIDE)


def solution(mesh):
    placed = (P("aux", None, "row", "col"), P("col", None), P("aux", None, None))
    return jax.shard_map(
        on_device, mesh=mesh, in_specs=placed, out_specs=P(("aux", "row"), "col"), check_vma=False
    )
```

time: 321 us -> 94.5 us (0.29)
  waiting for transfers between devices: 245 us -> 0 us
  Pallas kernels: 0 us -> 91.6 us
  local copies, waits for them, and re-layouts: 28.2 us -> 2.78 us
  matrix products: 24.5 us -> 0 us
  between operations: 13.2 us -> 0.01 us
  other arithmetic: 7.97 us -> 0 us
    all_gather x3 -> x0, waiting for transfers between devices: 154 us -> none  [the longest x2 130 us: one_function(): lax.all_gather(right_rows, 'row', axis=0, tiled=True)]
    pallas_call x0 -> x1, Pallas kernels: none -> 91.6 us  [on_device(): pl.pallas_call(kernel, out_shape=jax.ShapeDtypeStruct((NZ, ROWS, WIDE), F...]
    unnamed x4 -> x0, waiting for transfers between devices: 52.2 us -> none
    reduce_scatter x1 -> x0, waiting for transfers between devices: 38.7 us -> none  [on_device(): lax.psum_scatter(partial_k.astype(jnp.bfloat16), 'aux', scatter_dimension...]
    dot_general x3 -> x0, matrix products: 24.5 us -> none  [the longest x2 15.1 us: one_function(): lax.dot_general(left_rows, lax.all_gather(right_rows, 'row', axis=0, tile...]
    mul x2 -> x0, local copies, waits for them, and re-layouts: 18.7 us -> none  [on_device(): factors.reshape(local_count, aux_parts, row_len, tile_cols, TILE)]
    convert_element_type x3 -> x0, other arithmetic: 7.79 us -> none  [the longest x1 4.98 us: on_device(): partial_k.astype(jnp.bfloat16)]
    gather x1 -> x0, local copies, waits for them, and re-layouts: 3.39 us -> none  [on_device(): row_tiles = jnp.take(tile_mask, basis_rows, axis=1)]
  transfers between devices with their start and end apart: 5 -> 0, of which waited for: 5 -> 0; matrix products, arithmetic and copies ran while one was open for 1% -> 0% of each run, Pallas kernels for 0% -> 0%
where the time goes in v1:
time: 94.5 us; the launch traced here: 94.4 us
  Pallas kernels  91.6 us (97%)
  local copies, waits for them, and re-layouts  2.78 us (3%)
    pallas_call x1, Pallas kernels, on_device(): pl.pallas_call(kernel, out_shape=jax.ShapeDtypeStruct((NZ, ROWS, WIDE), F...  91.6 us
    reshape x1, local copies, waits for them, and re-layouts, on_device(): return out.transpose(1, 0, 2).reshape(ROWS, NZ * WIDE)  2.78 us

profile of v1, /device:TPU:2, one launch (start us, length us, event | category | flops | bytes accessed | tf_op | source)
XLA Modules:
  0.0 94.4 jit_solution(14160006579914603203)
XLA Ops:
  0.0 91.6 %exchange.1 = f32[4,160,640]{2,1,0:T(8,128)} custom-call(s32[2,80,80]{2,1,0:T(8,128)} %mask_ref.1, bf16[2,4,160,2560]{3,2,1,0:T(8,128)(2,1)} %factors_ref.1, bf16[2560,512]{1,0:T(8,128)(2,1)} %orbitals_ref.1), custom_call_target="tpu_custom_call" | custom-call | flops 7000000000 | bytes 12000000 | tf_op jit(solution)/shard_map/exchange/pallas_call | solution.py:271
  91.6 2.8 %copy.5 = f32[4,20,8,640]{3,2,0,1:T(8,128)} copy(f32[4,20,8,640]{3,2,1,0:T(8,128)} %bitcast.3) | data formatting | bytes 3276800 | tf_op jit(solution)/shard_map/reshape | solution.py:303

commit v2 on v1

v2 whole, which is shorter than its diff:
```python
import jax
import jax.numpy as jnp
from jax import lax
from jax.experimental import pallas as pl
from jax.experimental.pallas import tpu as pltpu
from jax.sharding import PartitionSpec as P

NB = 10240
TILE = 128
MESH = pl.DeviceIdType.MESH
BF = jnp.bfloat16
F32 = jnp.float32
NT = (((1,), (1,)), ((), ()))
NX, NY, NZ = 4, 4, 4
ROWS, HALF, OCC = 160, 80, 512
WIDE = NY * ROWS
COLS = NB // 4
PARTS = 4
PART = 2 * OCC // PARTS
Y_FIRST = (3,)
CUT = 384
SPLIT = (2, 3)
N_SEMS = 12 + 23 * PARTS + 6 * len(Y_FIRST) + 24 + 6 * len(SPLIT)


def kernel(mask_hbm, factors_ref, orbitals_ref, out_ref,
           fbuf, cbuf, mask_ref, mexp, masked, give, keep, got_a, put_b, got_b, panels, left, prod, turned, natural, gathered,
           far, near, got_far, got_near, held, in_sem, send_sem, recv_sem):
    x = lax.axis_index("aux")
    row = lax.axis_index("row")
    col = lax.axis_index("col")
    zh, y = lax.div(row, NY), lax.rem(row, NY)
    core_col = col + 1 - 2 * lax.rem(col, 2)
    pair_col = lax.rem(col + 2, 4)
    cross_col = 3 - col

    def at_x(d):
        return lax.rem(x + d + NX, NX)

    def at_y(d):
        return lax.rem(y + d + NY, NY)

    def at_z(d):
        return lax.rem(zh + d + NZ, NZ)

    side = 2 * lax.div(col, 2) - 1
    core = {"col": core_col}
    pair = {"col": pair_col}
    next_chip = {"row": at_z(side) * NY + y, "col": pair_col}
    y_dev = {d: {"row": zh * NY + at_y(d)} for d in (1, -1)}
    z_near, z_far = {"row": at_z(side) * NY + y}, {"row": at_z(-side) * NY + y}
    x_dev = {d: {"aux": at_x(d)} for d in (1, -1)}
    layers = (zh, at_z(side), at_z(-side), at_z(2))

    barrier = pltpu.get_barrier_semaphore()
    partners = [core, pair, next_chip, y_dev[1], y_dev[-1], z_near, z_far, x_dev[1], x_dev[-1]]
    for partner in partners:
        pl.semaphore_signal(barrier, inc=1, device_id=partner, device_id_type=MESH)

    order = (core_col, col, cross_col, pair_col)
    flags_in = pltpu.make_async_copy(mask_hbm, mask_ref, in_sem.at[9])
    flags_in.start()
    loads = {}
    load = pltpu.make_async_copy(orbitals_ref, cbuf, in_sem.at[8])
    load.start()
    for n, (q, s) in enumerate(((0, 0), (0, 1), (1, 0), (1, 1), (0, 2), (0, 3), (1, 2), (1, 3))):
        piece = pltpu.make_async_copy(factors_ref.at[q, order[s]], fbuf.at[q, order[s]], in_sem.at[n])
        piece.start()
        loads[q, s] = piece

    flags_in.wait()
    pick_row = lax.broadcasted_iota(jnp.int32, (64, 80), 0)
    pick_col = lax.broadcasted_iota(jnp.int32, (64, 80), 1)
    tile_row = (pick_row // 16) * (COLS // TILE) + (row * (ROWS // 32) + pick_row % 8) // (TILE // 32)
    spread_row = lax.broadcasted_iota(jnp.int32, (80, COLS), 0)
    spread_col = lax.broadcasted_iota(jnp.int32, (80, COLS), 1)
    spread = (spread_row == col * (COLS // TILE) + spread_col // TILE).astype(BF)
    flags = jnp.zeros((64, 80), F32)
    for q in range(2):
        pick = ((pick_col == tile_row) & ((pick_row % 16) // 8 == q)).astype(BF)
        flags = flags + jnp.dot(pick, mask_ref[q].astype(F32).astype(BF), preferred_element_type=F32)
    mexp[...] = jnp.dot(flags.astype(BF), spread, preferred_element_type=F32).reshape(4, 16, COLS)

    sends = []
    used = [0]

    def sem():
        used[0] += 1
        return used[0] - 1

    def send(src, dst, index, to):
        copy = pltpu.make_async_remote_copy(
            src_ref=src, dst_ref=dst, send_sem=send_sem.at[index], recv_sem=recv_sem.at[index],
            device_id=to, device_id_type=MESH)
        copy.start()
        sends.append(copy)

    seen = set()

    def arrived(dst, index, to):
        if index in seen:
            return
        seen.add(index)
        pltpu.make_async_remote_copy(
            src_ref=dst, dst_ref=dst, send_sem=send_sem.at[index], recv_sem=recv_sem.at[index],
            device_id=to, device_id_type=MESH).wait_recv()

    s_a = {(q, s): sem() for q in range(2) for s in range(2)}
    s_b, s_core, s_cross = ({p: sem() for p in range(PARTS)} for _ in range(3))
    s_in = {(n, p): sem() for n in range(NZ) for p in range(PARTS)}
    s_fy = {(n, p, d): sem() for n in range(2) for p in Y_FIRST for d in (1, -1, 2)}
    s_y1, s_y2 = (
        {(n, p, d): sem() for n in range(NZ) for p in range(PARTS) for d in (1, -1)} for _ in range(2))
    cuts = {n: (pl.ds(0, CUT), pl.ds(CUT, WIDE - CUT)) if n in SPLIT else (pl.ds(0, WIDE),) for n in range(NZ)}
    s_far = {(n, i, d): sem() for n in range(NZ) for i in range(len(cuts[n])) for d in (1, -1)}
    s_near = {(n, i, d, h): sem() for n in range(NZ) for i in range(len(cuts[n])) for d in (1, -1) for h in range(2)}
    lanes = [pl.ds(p * PART, PART) for p in range(PARTS)]
    parts_of = [range(q * PARTS // 2, (q + 1) * PARTS // 2) for q in range(2)]
    everything = pl.ds(0, ROWS)
    halves = {1: pl.ds(0, HALF), -1: pl.ds(HALF, HALF)}

    def partial_product(q, s):
        quarter = order[s]
        loads[q, s].wait()
        for g in range(ROWS // 32):
            flag_row = mexp[quarter, pl.ds(8 * q + g, 1), :].astype(BF)
            masked[pl.ds(32 * g, 32), :] = fbuf[q, quarter, pl.ds(32 * g, 32), :] * flag_row
        return jnp.dot(masked[...], cbuf[...], preferred_element_type=F32)

    def give_core(q, n):
        give[q, n] = partial_product(q, 2 * n).astype(BF)
        send(give.at[q, n], got_a.at[q, n], s_a[q, n], core)

    def give_pair(q):
        arrived(got_a.at[q, 0], s_a[q, 0], core)
        put_b[q] = (keep[q, 0] + got_a[q, 0].astype(F32)).astype(BF)
        for p in parts_of[q]:
            within = pl.ds((p - parts_of[q][0]) * PART, PART)
            send(put_b.at[q, everything, within], got_b.at[q, everything, within], s_b[p], pair)

    def block(n, at, p, rows=everything):
        return panels.at[layers[n], at, rows, lanes[p]]

    def finish_rows(p):
        q = p * 2 // PARTS
        within = pl.ds((p - parts_of[q][0]) * PART, PART)
        if p == parts_of[q][0]:
            arrived(got_a.at[q, 1], s_a[q, 1], core)
        arrived(got_b.at[q, everything, within], s_b[p], pair)
        rows = (keep[q, 1, :, within] + got_a[q, 1, :, within].astype(F32) + got_b[q, :, within].astype(F32)).astype(BF)
        left[pair_col, :, lanes[p]] = rows
        mine = left.at[pair_col, everything, lanes[p]]
        send(mine, block(0, y, p), s_in[0, p], pair)
        send(mine, block(0, y, p), s_in[1, p], next_chip)
        send(mine, mine, s_cross[p], core)

    load.wait()
    give_value = partial_product(0, 0).astype(BF)
    give[0, 0] = give_value
    pl.semaphore_wait(barrier, len(partners))
    send(give.at[0, 0], got_a.at[0, 0], s_a[0, 0], core)
    keep[0, 0] = partial_product(0, 1)
    give_core(1, 0)
    give_pair(0)
    keep[1, 0] = partial_product(1, 1)
    give_core(0, 1)
    give_pair(1)
    keep[0, 1] = partial_product(0, 3)
    give_core(1, 1)
    keep[1, 1] = partial_product(1, 3)

    def own_step(p):
        arrived(block(0, y, p), s_in[0, p], pair)
        send(block(0, y, p), block(0, y, p), s_in[2, p], z_near)
        left[col, :, lanes[p]] = panels[zh, y, :, lanes[p]]
        mine = left.at[col, everything, lanes[p]]
        send(mine, mine, s_core[p], core)

    def next_step(p):
        arrived(block(1, y, p), s_in[1, p], next_chip)
        send(block(1, y, p), block(1, y, p), s_in[3, p], z_far)

    def land(n, p):
        if n >= 2:
            arrived(block(n, y, p), s_in[n, p], z_far if n == 2 else z_near)

    def along_y1(n, p):
        land(n, p)
        for d in (1, -1):
            send(block(n, y, p), block(n, y, p), s_y1[n, p, d], y_dev[d])

    def along_y2(n, p):
        for d in (1, -1):
            arrived(block(n, at_y(-d), p), s_y1[n, p, d], y_dev[-d])
            part = block(n, at_y(-d), p, halves[d])
            send(part, part, s_y2[n, p, d], y_dev[d])

    def forward(n, p, steps):
        for d in steps:
            if d == 2:
                end_y2(n, p)
            whole = block(n, at_y(d), p)
            send(whole, whole, s_fy[n, p, d], z_near if n == 0 else z_far)

    def end_y2(n, p):
        for d in (1, -1):
            arrived(block(n, at_y(2), p, halves[d]), s_y2[n, p, d], y_dev[-d])

    def end_left():
        for p in range(PARTS):
            arrived(left.at[cross_col, everything, lanes[p]], s_cross[p], core)
            arrived(left.at[core_col, everything, lanes[p]], s_core[p], core)

    def ready(n, last):
        end_left()
        for p in range(PARTS):
            if n >= 2 and p in Y_FIRST:
                land(n, p)
                for d in (1, -1, 2) if last else (1, -1):
                    arrived(block(n, at_y(d), p), s_fy[n - 2, p, d], z_far if n == 2 else z_near)
            else:
                for d in (1, -1):
                    arrived(block(n, at_y(-d), p), s_y1[n, p, d], y_dev[-d])
                if last:
                    end_y2(n, p)

    def columns(n):
        return pl.ds(pl.multiple_of(layers[n] * WIDE, TILE), WIDE)

    def product(n, i=0):
        last = i == len(cuts[n]) - 1
        cut = cuts[n][i]
        ready(n, last)
        if n in SPLIT:
            slot = SPLIT.index(n)
            for at, d in ((3, 2),) if last else ((0, 0), (1, 1), (2, -1)):
                gathered[slot, pl.ds(at * ROWS, ROWS)] = panels[layers[n], at_y(d)]
            right = gathered[slot, cut]
        else:
            right = panels[layers[n]].reshape(WIDE, 2 * OCC)
        value = lax.dot_general(
            left[...].reshape(4 * ROWS, 2 * OCC), right, NT, preferred_element_type=F32)
        prod[:, :, cut] = value.reshape(4, ROWS, cut.size)
        far[n, :, cut] = prod[at_x(2), :, cut].astype(BF)
        for d in (1, -1):
            send(far.at[n, halves[d], cut], got_far.at[n, 0 if d == 1 else 1, pl.ds(0, HALF), cut], s_far[n, i, d], x_dev[d])
        for d in (1, -1):
            slot = 0 if d == 1 else 1
            mine, other = halves[d], halves[-d]
            near[n, slot, other, cut] = prod[at_x(d), other, cut].astype(BF)
            held[n, slot, :, cut] = prod[at_x(d), mine, cut]
            send(near.at[n, slot, other, cut], got_near.at[n, slot, other, cut], s_near[n, i, d, 1], x_dev[d])
        if n in SPLIT:
            turned[SPLIT.index(n), :, cut] = prod[x, :, cut]
        else:
            out_ref[:, columns(n)] = prod[x]

    def pass_on(n, i=0):
        cut = cuts[n][i]
        for d in (1, -1):
            slot = 0 if d == 1 else 1
            mine = halves[d]
            arrived(got_far.at[n, slot, pl.ds(0, HALF), cut], s_far[n, i, d], x_dev[-d])
            near[n, slot, mine, cut] = (held[n, slot, :, cut] + got_far[n, slot, :, cut].astype(F32)).astype(BF)
            send(near.at[n, slot, mine, cut], got_near.at[n, slot, mine, cut], s_near[n, i, d, 0], x_dev[d])

    def finish(n, i=0):
        cut = cuts[n][i]
        for d in (1, -1):
            slot = 0 if d == 1 else 1
            arrived(got_near.at[n, slot, halves[d], cut], s_near[n, i, d, 0], x_dev[-d])
            arrived(got_near.at[n, slot, halves[-d], cut], s_near[n, i, d, 1], x_dev[-d])
        total = got_near[n, 0, :, cut].astype(F32) + got_near[n, 1, :, cut].astype(F32)
        if n not in SPLIT:
            out_ref[:, columns(n)] += total
            return
        at = SPLIT.index(n)
        turned[at, :, cut] += total
        if i == len(cuts[n]) - 1:
            for v in range(NY):
                @pl.when(y == v)
                def _(v=v):
                    for place, d in enumerate((0, 1, -1, 2)):
                        natural[:, pl.ds((v + d) % NY * ROWS, ROWS)] = turned[at, :, pl.ds(place * ROWS, ROWS)]
            out_ref[:, columns(n)] = natural[...]

    finish_rows(0)
    finish_rows(1)
    finish_rows(2)
    next_step(0)
    along_y1(1, 0)
    finish_rows(3)
    next_step(1)
    along_y1(1, 1)
    own_step(0)
    next_step(2)
    along_y1(1, 2)
    along_y2(1, 0)
    own_step(1)
    next_step(3)
    along_y1(1, 3)
    along_y2(1, 1)
    along_y1(0, 0)
    own_step(2)
    along_y2(1, 2)
    along_y1(0, 1)
    along_y2(1, 3)
    forward(1, 3, (1, -1))
    along_y1(0, 2)
    own_step(3)
    along_y1(0, 3)
    along_y2(0, 0)
    along_y2(0, 1)
    product(1)
    forward(1, 3, (2,))
    along_y2(0, 2)
    along_y2(0, 3)
    forward(0, 3, (1, -1))
    along_y1(3, 0)
    along_y1(3, 1)
    along_y1(3, 2)
    along_y1(2, 0)
    along_y1(2, 1)
    pass_on(1)
    along_y1(2, 2)
    product(0)
    forward(0, 3, (2,))
    along_y2(3, 0)
    finish(1)
    along_y2(3, 1)
    product(3, 0)
    pass_on(0)
    along_y2(3, 2)
    along_y2(2, 0)
    along_y2(2, 1)
    pass_on(3, 0)
    along_y2(2, 2)
    product(2, 0)
    product(3, 1)
    finish(0)
    finish(3, 0)
    product(2, 1)
    pass_on(2, 0)
    pass_on(3, 1)
    pass_on(2, 1)
    finish(2, 0)
    finish(3, 1)
    finish(2, 1)
    for copy in sends:
        copy.wait_send()


def on_device(factors, orbitals, tile_mask):
    vmem = pl.BlockSpec(memory_space=pltpu.VMEM)
    hbm = pl.BlockSpec(memory_space=pl.ANY)
    return pl.pallas_call(
        kernel,
        out_shape=jax.ShapeDtypeStruct((ROWS, COLS), F32),
        in_specs=[hbm, hbm, hbm],
        out_specs=vmem,
        scratch_shapes=[
            pltpu.VMEM((2, 4, ROWS, COLS), BF),
            pltpu.VMEM((COLS, OCC), BF),
            pltpu.VMEM((2, NB // TILE, NB // TILE), jnp.int32),
            pltpu.VMEM((4, 16, COLS), F32),
            pltpu.VMEM((ROWS, COLS), BF),
            pltpu.VMEM((2, 2, ROWS, OCC), BF),
            pltpu.VMEM((2, 2, ROWS, OCC), F32),
            pltpu.VMEM((2, 2, ROWS, OCC), BF),
            pltpu.VMEM((2, ROWS, OCC), BF),
            pltpu.VMEM((2, ROWS, OCC), BF),
            pltpu.VMEM((NZ, NY, ROWS, 2 * OCC), BF),
            pltpu.VMEM((4, ROWS, 2 * OCC), BF),
            pltpu.VMEM((4, ROWS, WIDE), F32),
            pltpu.VMEM((max(1, len(SPLIT)), ROWS, WIDE), F32),
            pltpu.VMEM((ROWS, WIDE), F32),
            pltpu.VMEM((max(1, len(SPLIT)), WIDE, 2 * OCC), BF),
            pltpu.VMEM((NZ, ROWS, WIDE), BF),
            pltpu.VMEM((NZ, 2, ROWS, WIDE), BF),
            pltpu.VMEM((NZ, 2, HALF, WIDE), BF),
            pltpu.VMEM((NZ, 2, ROWS, WIDE), BF),
            pltpu.VMEM((NZ, 2, HALF, WIDE), F32),
            pltpu.SemaphoreType.DMA((10,)),
            pltpu.SemaphoreType.DMA((N_SEMS,)),
            pltpu.SemaphoreType.DMA((N_SEMS,)),
        ],
        compiler_params=pltpu.CompilerParams(
            collective_id=0, has_side_effects=True, vmem_limit_bytes=56 * 2**20),
        cost_estimate=pl.CostEstimate(flops=7 * 10**9, bytes_accessed=12 * 10**6, transcendentals=0),
        name="exchange",
    )(tile_mask, factors, orbitals)


def solution(mesh):
    placed = (P("aux", None, "row", "col"), P("col", None), P("aux", None, None))
    return jax.shard_map(
        on_device, mesh=mesh, in_specs=placed, out_specs=P(("aux", "row"), "col"), check_vma=False
    )
```

time: 94.5 us -> 73.1 us (0.77)
  Pallas kernels: 91.6 us -> 69.8 us
    pallas_call x1, Pallas kernels: 91.6 us -> 69.8 us  [on_device(): pl.pallas_call(kernel, out_shape=jax.ShapeDtypeStruct((ROWS, COLS), F32),...]
    reshape x1 -> x0, local copies, waits for them, and re-layouts: 2.78 us -> none  [on_device(): return out.transpose(1, 0, 2).reshape(ROWS, NZ * WIDE)]
    unnamed x0 -> x1, local copies, waits for them, and re-layouts: none -> 2.71 us
where the time goes in v2:
time: 73.1 us; the launch traced here: 72.5 us
  Pallas kernels  69.8 us (95%)
  local copies, waits for them, and re-layouts  2.71 us (4%)
    pallas_call x1, Pallas kernels, on_device(): pl.pallas_call(kernel, out_shape=jax.ShapeDtypeStruct((ROWS, COLS), F32),...  69.8 us
    unnamed x1, local copies, waits for them, and re-layouts  2.71 us

profile of v2, /device:TPU:2, one launch (start us, length us, event | category | flops | bytes accessed | tf_op | source)
XLA Modules:
  0.0 72.5 jit_solution(9872268409004290537)
XLA Ops:
  0.0 69.8 %exchange.1 = f32[160,2560]{1,0:T(8,128)} custom-call(s32[2,80,80]{2,1,0:T(8,128)} %mask_hbm.1, bf16[2,4,160,2560]{3,2,1,0:T(8,128)(2,1)} %factors_ref.1, bf16[2560,512]{1,0:T(8,128)(2,1)} %orbitals_ref.1), custom_call_target="tpu_custom_call" | custom-call | flops 7000000000 | bytes 12000000 | tf_op jit(solution)/shard_map/exchange/pallas_call | solution.py:356
  69.8 2.7 %copy.5 = f32[160,2560]{1,0:T(8,128)} copy(f32[160,2560]{1,0:T(8,128)} %exchange.1) | data formatting | bytes 3276800

commit v3 on v2

--- a/solution.py
+++ b/solution.py
@@ -18,9 +18,8 @@
 PARTS = 4
 PART = 2 * OCC // PARTS
 Y_FIRST = (3,)
-CUT = 384
-SPLIT = (2, 3)
-N_SEMS = 12 + 23 * PARTS + 6 * len(Y_FIRST) + 24 + 6 * len(SPLIT)
+CUTS = ((640,), (640,), (384, 256), (384, 256))
+N_SEMS = 12 + 23 * PARTS + 6 * len(Y_FIRST) + 6 * sum(map(len, CUTS))
 
 
 def kernel(mask_hbm, factors_ref, orbitals_ref, out_ref,
@@ -111,7 +110,7 @@
     s_fy = {(n, p, d): sem() for n in range(2) for p in Y_FIRST for d in (1, -1, 2)}
     s_y1, s_y2 = (
         {(n, p, d): sem() for n in range(NZ) for p in range(PARTS) for d in (1, -1)} for _ in range(2))
-    cuts = {n: (pl.ds(0, CUT), pl.ds(CUT, WIDE - CUT)) if n in SPLIT else (pl.ds(0, WIDE),) for n in range(NZ)}
+    cuts = [[pl.ds(sum(c[:i]), c[i]) for i in range(len(c))] for c in CUTS]
     s_far = {(n, i, d): sem() for n in range(NZ) for i in range(len(cuts[n])) for d in (1, -1)}
     s_near = {(n, i, d, h): sem() for n in range(NZ) for i in range(len(cuts[n])) for d in (1, -1) for h in range(2)}
     lanes = [pl.ds(p * PART, PART) for p in range(PARTS)]
@@ -169,7 +168,10 @@
     give_core(1, 1)
     keep[1, 1] = partial_product(1, 3)
 
+    left_done = set()
+
     def own_step(p):
+        left_done.add(p)
         arrived(block(0, y, p), s_in[0, p], pair)
         send(block(0, y, p), block(0, y, p), s_in[2, p], z_near)
         left[col, :, lanes[p]] = panels[zh, y, :, lanes[p]]
@@ -211,31 +213,43 @@
             arrived(left.at[cross_col, everything, lanes[p]], s_cross[p], core)
             arrived(left.at[core_col, everything, lanes[p]], s_core[p], core)
 
-    def ready(n, last):
+    placed = (0, 1, -1, 2)
+
+    def blocks_of(n, i):
+        first = cuts[n][i].start
+        return [k for k in range(NY) if k * ROWS < first + cuts[n][i].size and (k + 1) * ROWS > first]
+
+    placed_blocks, cuts_done = set(), set()
+
+    def ready(n, i):
+        assert len(left_done) == PARTS
         end_left()
-        for p in range(PARTS):
-            if n >= 2 and p in Y_FIRST:
-                land(n, p)
-                for d in (1, -1, 2) if last else (1, -1):
-                    arrived(block(n, at_y(d), p), s_fy[n - 2, p, d], z_far if n == 2 else z_near)
-            else:
-                for d in (1, -1):
-                    arrived(block(n, at_y(-d), p), s_y1[n, p, d], y_dev[-d])
-                if last:
+        for k in range(NY) if len(cuts[n]) == 1 else blocks_of(n, i):
+            for p in range(PARTS):
+                if k == 0:
+                    if n < 2:
+                        arrived(block(n, y, p), s_in[n, p], pair if n == 0 else next_chip)
+                    land(n, p)
+                elif n >= 2 and p in Y_FIRST:
+                    arrived(block(n, at_y(placed[k]), p), s_fy[n - 2, p, placed[k]], z_far if n == 2 else z_near)
+                elif k == 3:
                     end_y2(n, p)
+                else:
+                    arrived(block(n, at_y(placed[k]), p), s_y1[n, p, -placed[k]], y_dev[placed[k]])
 
     def columns(n):
         return pl.ds(pl.multiple_of(layers[n] * WIDE, TILE), WIDE)
 
     def product(n, i=0):
-        last = i == len(cuts[n]) - 1
         cut = cuts[n][i]
-        ready(n, last)
-        if n in SPLIT:
-            slot = SPLIT.index(n)
-            for at, d in ((3, 2),) if last else ((0, 0), (1, 1), (2, -1)):
-                gathered[slot, pl.ds(at * ROWS, ROWS)] = panels[layers[n], at_y(d)]
-            right = gathered[slot, cut]
+        ready(n, i)
+        if len(cuts[n]) > 1:
+            for k in blocks_of(n, i):
+                if (n, k) in placed_blocks:
+                    continue
+                placed_blocks.add((n, k))
+                gathered[n, pl.ds(k * ROWS, ROWS)] = panels[layers[n], at_y(placed[k])]
+            right = gathered[n, cut]
         else:
             right = panels[layers[n]].reshape(WIDE, 2 * OCC)
         value = lax.dot_general(
@@ -250,8 +264,8 @@
             near[n, slot, other, cut] = prod[at_x(d), other, cut].astype(BF)
             held[n, slot, :, cut] = prod[at_x(d), mine, cut]
             send(near.at[n, slot, other, cut], got_near.at[n, slot, other, cut], s_near[n, i, d, 1], x_dev[d])
-        if n in SPLIT:
-            turned[SPLIT.index(n), :, cut] = prod[x, :, cut]
+        if len(cuts[n]) > 1:
+            turned[n, :, cut] = prod[x, :, cut]
         else:
             out_ref[:, columns(n)] = prod[x]
 
@@ -271,18 +285,20 @@
             arrived(got_near.at[n, slot, halves[d], cut], s_near[n, i, d, 0], x_dev[-d])
             arrived(got_near.at[n, slot, halves[-d], cut], s_near[n, i, d, 1], x_dev[-d])
         total = got_near[n, 0, :, cut].astype(F32) + got_near[n, 1, :, cut].astype(F32)
-        if n not in SPLIT:
+        if len(cuts[n]) == 1:
             out_ref[:, columns(n)] += total
             return
-        at = SPLIT.index(n)
-        turned[at, :, cut] += total
-        if i == len(cuts[n]) - 1:
-            for v in range(NY):
-                @pl.when(y == v)
-                def _(v=v):
-                    for place, d in enumerate((0, 1, -1, 2)):
-                        natural[:, pl.ds((v + d) % NY * ROWS, ROWS)] = turned[at, :, pl.ds(place * ROWS, ROWS)]
-            out_ref[:, columns(n)] = natural[...]
+        turned[n, :, cut] += total
+        cuts_done.add((n, i))
+        full = [k for k in range(NY) if k in blocks_of(n, i) and all(
+            (n, j) in cuts_done for j in range(len(cuts[n])) if k in blocks_of(n, j))]
+        for v in range(NY):
+            @pl.when(y == v)
+            def _(v=v):
+                for k in full:
+                    natural[n, :, pl.ds((v + placed[k]) % NY * ROWS, ROWS)] = turned[n, :, pl.ds(k * ROWS, ROWS)]
+        if all((n, j) in cuts_done for j in range(len(cuts[n]))):
+            out_ref[:, columns(n)] = natural[n]
 
     finish_rows(0)
     finish_rows(1)
@@ -292,56 +308,56 @@
     finish_rows(3)
     next_step(1)
     along_y1(1, 1)
-    own_step(0)
     next_step(2)
     along_y1(1, 2)
+    own_step(0)
+    next_step(3)
+    along_y1(1, 3)
+    along_y1(0, 0)
     along_y2(1, 0)
     own_step(1)
-    next_step(3)
-    along_y1(1, 3)
     along_y2(1, 1)
-    along_y1(0, 0)
+    along_y1(0, 1)
+    along_y2(1, 2)
     own_step(2)
-    along_y2(1, 2)
-    along_y1(0, 1)
     along_y2(1, 3)
+    along_y1(0, 2)
     forward(1, 3, (1, -1))
-    along_y1(0, 2)
     own_step(3)
     along_y1(0, 3)
     along_y2(0, 0)
     along_y2(0, 1)
     product(1)
-    forward(1, 3, (2,))
     along_y2(0, 2)
     along_y2(0, 3)
     forward(0, 3, (1, -1))
+    along_y1(3, 2)
     along_y1(3, 0)
     along_y1(3, 1)
-    along_y1(3, 2)
     along_y1(2, 0)
+    pass_on(1)
     along_y1(2, 1)
-    pass_on(1)
+    product(0)
+    along_y2(3, 0)
     along_y1(2, 2)
-    product(0)
-    forward(0, 3, (2,))
-    along_y2(3, 0)
-    finish(1)
-    along_y2(3, 1)
     product(3, 0)
     pass_on(0)
     along_y2(3, 2)
+    forward(1, 3, (2,))
     along_y2(2, 0)
+    along_y2(3, 1)
+    pass_on(3, 0)
     along_y2(2, 1)
-    pass_on(3, 0)
+    finish(1)
+    forward(0, 3, (2,))
     along_y2(2, 2)
     product(2, 0)
     product(3, 1)
-    finish(0)
-    finish(3, 0)
     product(2, 1)
     pass_on(2, 0)
+    finish(3, 0)
     pass_on(3, 1)
+    finish(0)
     pass_on(2, 1)
     finish(2, 0)
     finish(3, 1)
@@ -352,10 +368,10 @@
 
 def on_device(factors, orbitals, tile_mask):
     vmem = pl.BlockSpec(memory_space=pltpu.VMEM)
-    hbm = pl.BlockSpec(memory_space=pl.ANY)
+    hbm = pl.BlockSpec(memory_space=pltpu.HBM)
     return pl.pallas_call(
         kernel,
-        out_shape=jax.ShapeDtypeStruct((ROWS, COLS), F32),
+        out_shape=pltpu.VMEM((ROWS, COLS), F32),
         in_specs=[hbm, hbm, hbm],
         out_specs=vmem,
         scratch_shapes=[
@@ -372,9 +388,9 @@
             pltpu.VMEM((NZ, NY, ROWS, 2 * OCC), BF),
             pltpu.VMEM((4, ROWS, 2 * OCC), BF),
             pltpu.VMEM((4, ROWS, WIDE), F32),
-            pltpu.VMEM((max(1, len(SPLIT)), ROWS, WIDE), F32),
-            pltpu.VMEM((ROWS, WIDE), F32),
-            pltpu.VMEM((max(1, len(SPLIT)), WIDE, 2 * OCC), BF),
+            pltpu.VMEM((NZ, ROWS, WIDE), F32),
+            pltpu.VMEM((NZ, ROWS, WIDE), F32),
+            pltpu.VMEM((NZ, WIDE, 2 * OCC), BF),
             pltpu.VMEM((NZ, ROWS, WIDE), BF),
             pltpu.VMEM((NZ, 2, ROWS, WIDE), BF),
             pltpu.VMEM((NZ, 2, HALF, WIDE), BF),
@@ -385,10 +401,10 @@
             pltpu.SemaphoreType.DMA((N_SEMS,)),
         ],
         compiler_params=pltpu.CompilerParams(
-            collective_id=0, has_side_effects=True, vmem_limit_bytes=56 * 2**20),
+            collective_id=0, has_side_effects=True, vmem_limit_bytes=54 * 2**20),
         cost_estimate=pl.CostEstimate(flops=7 * 10**9, bytes_accessed=12 * 10**6, transcendentals=0),
         name="exchange",
-    )(tile_mask, factors, orbitals)
+    )(pltpu.with_memory_space_constraint(tile_mask, pltpu.HBM), factors, orbitals)
 
 
 def solution(mesh):

time: 73.1 us -> 70.9 us (0.970)
  local copies, waits for them, and re-layouts: 2.71 us -> 1.17 us
    unnamed x1, local copies, waits for them, and re-layouts: 2.71 us -> 1.17 us
where the time goes in v3:
time: 70.9 us; the launch traced here: 70.8 us
  Pallas kernels  69.6 us (98%)
  local copies, waits for them, and re-layouts  1.17 us (2%)
    pallas_call x1, Pallas kernels, on_device(): pl.pallas_call(kernel, out_shape=pltpu.VMEM((ROWS, COLS), F32), in_specs=...  69.6 us

profile of v3, /device:TPU:2, one launch (start us, length us, event | category | flops | bytes accessed | tf_op | source)
XLA Modules:
  0.0 70.8 jit_solution(787773114863616854)
XLA Ops:
  0.0 69.6 %exchange.1 = f32[160,2560]{1,0:T(8,128)S(1)} custom-call(s32[2,80,80]{2,1,0:T(8,128)} %mask_hbm.1, bf16[2,4,160,2560]{3,2,1,0:T(8,128)(2,1)} %factors_ref.1, bf16[2560,512]{1,0:T(8,128)(2,1)} %orbitals_ref.1), custom_call_target="tpu_custom_call" | custom-call | flops 7000000000 | bytes 12000000 | tf_op jit(solution)/shard_map/exchange/pallas_call | solution.py:372
  69.6 1.2 %copy.5 = f32[160,2560]{1,0:T(8,128)} copy(f32[160,2560]{1,0:T(8,128)S(1)} %exchange.1) | data formatting | bytes 3276800

commit v4 on v3

--- a/solution.py
+++ b/solution.py
@@ -191,22 +191,27 @@
         for d in (1, -1):
             send(block(n, y, p), block(n, y, p), s_y1[n, p, d], y_dev[d])
 
+    def turn(n, p):
+        return -1 if (p + n + n // 2) % 2 else 1
+
     def along_y2(n, p):
-        for d in (1, -1):
-            arrived(block(n, at_y(-d), p), s_y1[n, p, d], y_dev[-d])
-            part = block(n, at_y(-d), p, halves[d])
-            send(part, part, s_y2[n, p, d], y_dev[d])
+        d = turn(n, p)
+        whole = block(n, at_y(-d), p)
+        arrived(whole, s_y1[n, p, d], y_dev[-d])
+        send(whole, whole, s_y2[n, p, d], y_dev[d])
+
+    def end_y2(n, p):
+        d = turn(n, p)
+        arrived(block(n, at_y(2), p), s_y2[n, p, d], y_dev[-d])
 
     def forward(n, p, steps):
         for d in steps:
+            whole = block(n, at_y(d), p)
             if d == 2:
                 end_y2(n, p)
-            whole = block(n, at_y(d), p)
+            else:
+                arrived(whole, s_y1[n, p, -d], y_dev[d])
             send(whole, whole, s_fy[n, p, d], z_near if n == 0 else z_far)
-
-    def end_y2(n, p):
-        for d in (1, -1):
-            arrived(block(n, at_y(2), p, halves[d]), s_y2[n, p, d], y_dev[-d])
 
     def end_left():
         for p in range(PARTS):
@@ -310,57 +315,57 @@
     along_y1(1, 1)
     next_step(2)
     along_y1(1, 2)
+    along_y2(1, 0)
     own_step(0)
     next_step(3)
     along_y1(1, 3)
-    along_y1(0, 0)
-    along_y2(1, 0)
     own_step(1)
+    along_y1(0, 1)
     along_y2(1, 1)
-    along_y1(0, 1)
     along_y2(1, 2)
     own_step(2)
+    along_y1(0, 2)
     along_y2(1, 3)
-    along_y1(0, 2)
     forward(1, 3, (1, -1))
     own_step(3)
+    along_y1(0, 0)
     along_y1(0, 3)
+    along_y2(0, 1)
+    along_y2(0, 2)
+    product(1)
     along_y2(0, 0)
-    along_y2(0, 1)
-    product(1)
-    along_y2(0, 2)
     along_y2(0, 3)
+    along_y1(3, 0)
+    along_y1(3, 2)
+    along_y1(3, 1)
     forward(0, 3, (1, -1))
-    along_y1(3, 2)
-    along_y1(3, 0)
-    along_y1(3, 1)
     along_y1(2, 0)
     pass_on(1)
     along_y1(2, 1)
+    forward(1, 3, (2,))
     product(0)
-    along_y2(3, 0)
     along_y1(2, 2)
     product(3, 0)
     pass_on(0)
+    along_y2(3, 1)
+    along_y2(3, 0)
+    forward(0, 3, (2,))
     along_y2(3, 2)
-    forward(1, 3, (2,))
+    pass_on(3, 0)
     along_y2(2, 0)
-    along_y2(3, 1)
-    pass_on(3, 0)
+    product(2, 0)
     along_y2(2, 1)
-    finish(1)
-    forward(0, 3, (2,))
     along_y2(2, 2)
-    product(2, 0)
     product(3, 1)
     product(2, 1)
     pass_on(2, 0)
+    pass_on(3, 1)
+    pass_on(2, 1)
+    finish(1)
     finish(3, 0)
-    pass_on(3, 1)
-    finish(0)
-    pass_on(2, 1)
     finish(2, 0)
     finish(3, 1)
+    finish(0)
     finish(2, 1)
     for copy in sends:
         copy.wait_send()

time: 70.9 us -> 70.9 us (level)
  no operation moved by 1% of the time
where the time goes in v4:
time: 70.9 us; the launch traced here: 70.8 us
  Pallas kernels  69.6 us (98%)
  local copies, waits for them, and re-layouts  1.17 us (2%)
    pallas_call x1, Pallas kernels, on_device(): pl.pallas_call(kernel, out_shape=pltpu.VMEM((ROWS, COLS), F32), in_specs=...  69.6 us

profile of v4, /device:TPU:2, one launch (start us, length us, event | category | flops | bytes accessed | tf_op | source)
XLA Modules:
  0.0 70.8 jit_solution(12404460189070086542)
XLA Ops:
  0.0 69.6 %exchange.1 = f32[160,2560]{1,0:T(8,128)S(1)} custom-call(s32[2,80,80]{2,1,0:T(8,128)} %mask_hbm.1, bf16[2,4,160,2560]{3,2,1,0:T(8,128)(2,1)} %factors_ref.1, bf16[2560,512]{1,0:T(8,128)(2,1)} %orbitals_ref.1), custom_call_target="tpu_custom_call" | custom-call | flops 7000000000 | bytes 12000000 | tf_op jit(solution)/shard_map/exchange/pallas_call | solution.py:377
  69.6 1.2 %copy.5 = f32[160,2560]{1,0:T(8,128)} copy(f32[160,2560]{1,0:T(8,128)S(1)} %exchange.1) | data formatting | bytes 3276800

commit v5 on v4

--- a/solution.py
+++ b/solution.py
@@ -151,7 +151,9 @@
         mine = left.at[pair_col, everything, lanes[p]]
         send(mine, block(0, y, p), s_in[0, p], pair)
         send(mine, block(0, y, p), s_in[1, p], next_chip)
-        send(mine, mine, s_cross[p], core)
+        if p == parts_of[q][-1]:
+            both = left.at[pair_col, everything, pl.ds(q * OCC, OCC)]
+            send(both, both, s_cross[q], core)
 
     load.wait()
     give_value = partial_product(0, 0).astype(BF)
@@ -175,8 +177,10 @@
         arrived(block(0, y, p), s_in[0, p], pair)
         send(block(0, y, p), block(0, y, p), s_in[2, p], z_near)
         left[col, :, lanes[p]] = panels[zh, y, :, lanes[p]]
-        mine = left.at[col, everything, lanes[p]]
-        send(mine, mine, s_core[p], core)
+        q = p * 2 // PARTS
+        if all(other in left_done for other in parts_of[q]):
+            both = left.at[col, everything, pl.ds(q * OCC, OCC)]
+            send(both, both, s_core[q], core)
 
     def next_step(p):
         arrived(block(1, y, p), s_in[1, p], next_chip)
@@ -214,9 +218,10 @@
             send(whole, whole, s_fy[n, p, d], z_near if n == 0 else z_far)
 
     def end_left():
-        for p in range(PARTS):
-            arrived(left.at[cross_col, everything, lanes[p]], s_cross[p], core)
-            arrived(left.at[core_col, everything, lanes[p]], s_core[p], core)
+        for q in range(2):
+            both = pl.ds(q * OCC, OCC)
+            arrived(left.at[cross_col, everything, both], s_cross[q], core)
+            arrived(left.at[core_col, everything, both], s_core[q], core)
 
     placed = (0, 1, -1, 2)
 

time: 70.9 us -> 70.8 us (level)
  no operation moved by 1% of the time
where the time goes in v5:
time: 70.8 us
  Pallas kernels  69.6 us (98%)
  local copies, waits for them, and re-layouts  1.17 us (2%)
    pallas_call x1, Pallas kernels, on_device(): pl.pallas_call(kernel, out_shape=pltpu.VMEM((ROWS, COLS), F32), in_specs=...  69.6 us

profile of v5, /device:TPU:2, one launch (start us, length us, event | category | flops | bytes accessed | tf_op | source)
XLA Modules:
  0.0 70.8 jit_solution(583700782105612391)
XLA Ops:
  0.0 69.6 %exchange.1 = f32[160,2560]{1,0:T(8,128)S(1)} custom-call(s32[2,80,80]{2,1,0:T(8,128)} %mask_hbm.1, bf16[2,4,160,2560]{3,2,1,0:T(8,128)(2,1)} %factors_ref.1, bf16[2560,512]{1,0:T(8,128)(2,1)} %orbitals_ref.1), custom_call_target="tpu_custom_call" | custom-call | flops 7000000000 | bytes 12000000 | tf_op jit(solution)/shard_map/exchange/pallas_call | solution.py:382
  69.6 1.2 %copy.5 = f32[160,2560]{1,0:T(8,128)} copy(f32[160,2560]{1,0:T(8,128)S(1)} %exchange.1) | data formatting | bytes 3276800
